TPU v7x, 128 devices: a whole 4x4x4 slice. The times are simulated.
128 devices in a mesh: rep: 2 (over y_lo), tx: 8 (over x, y_hi), ty: 8 (over z, core).
Axes of the slice: x: 4, y: 4 (y_hi: 2, y_lo: 2; y = y_hi * 2 + y_lo), z: 4, core: 2. Of those that a mesh axis runs over, the one named last changes fastest.
Arguments:
- density: bfloat16 [2, 256, 512, 128], P('rep', 'tx', 'ty'), may hold values from -6 to 6
- kernel_one: bfloat16 [16, 4, 3, 3, 3], replicated, may hold values from -0.625 to 0.625
- kernel_two: bfloat16 [16, 16, 3, 3, 3], replicated, may hold values from -0.3125 to 0.3125
- cotangent: bfloat16 [2, 128, 256, 256], P('rep', 'tx', 'ty'), may hold values from -30 to 30
Outputs:
- features: bfloat16 [2, 128, 256, 256], P('rep', 'tx', 'ty')
- grad_one: float32 [16, 4, 3, 3, 3], replicated
- grad_two: float32 [16, 16, 3, 3, 3], replicated
All inputs are finite; a program needn't handle non-finite values.
Results may differ from a plain program's by a relative error of at most 0.015.
Values may be sent and summed in bfloat16 or wider, within the bound.
No kernel may reach another device: no remote copies, remote signals or barrier semaphores. Data moves between devices by JAX's collectives and lax.ppermute only.
A program may use at most 320 MiB of HBM per device.

v0:
```python
import jax
import jax.numpy as jnp
from jax import lax
from jax.sharding import PartitionSpec as P

CIN = 4
CH = 16
leak_slope = 0.3


def extended(value, sides, width):
    for axis, dim in sides:
        peers, length = (lax.axis_size(axis), value.shape[dim])
        up = [(i, (i + 1) % peers) for i in range(peers)]
        down = [(j, i) for i, j in up]
        last = lax.slice_in_dim(value, length - width, length, axis=dim)
        initial = lax.slice_in_dim(value, 0, width, axis=dim)
        before = lax.ppermute(last, axis, up)
        after = lax.ppermute(initial, axis, down)
        value = jnp.concatenate([before, value, after], axis=dim)
    return value


def convolve(lhs, rhs, specs):
    return lax.conv_general_dilated(
        lhs, rhs, (1, 1, 1), "VALID", dimension_numbers=specs, preferred_element_type=jnp.float32
    )


def depth_pad(field):
    return jnp.pad(field, ((0, 0), (0, 0), (1, 1), (0, 0), (0, 0)))


def pooling(field):
    s, c, d, x, y = field.shape
    blocks = field.astype(jnp.float32).reshape(s, c, d // 2, 2, x // 2, 2, y // 2, 2)
    return jnp.mean(blocks, axis=(3, 5, 7))


def upsample(field):
    s, c, d, x, y = field.shape
    grown = jnp.broadcast_to(field[:, :, :, None, :, None, :, None], (s, c, d, 2, x, 2, y, 2))
    return grown.reshape(s, c, 2 * d, 2 * x, 2 * y)


def unpack(field, channels):
    s, x, y, merged = field.shape
    return jnp.transpose(field.reshape(s, x, y, channels, merged // channels), (0, 3, 4, 1, 2))


def packing(field):
    s, c, d, x, y = field.shape
    return jnp.transpose(field, (0, 3, 4, 1, 2)).reshape(s, x, y, c * d)


def on_device(density, kernel_one, kernel_two, cotangent):
    forward = ("NCDHW", "OIDHW", "NCDHW")
    weight_form = ("CNDHW", "IODHW", "CNDHW")
    backward = ("NCDHW", "IODHW", "NCDHW")
    fine_width = 1
    grads = unpack(cotangent, CH)
    wide = unpack(extended(density, (("tx", 1), ("ty", 2)), fine_width), CIN)
    grad_rim = unpack(extended(cotangent, (("tx", 1), ("ty", 2)), 1), CH)
    padded = depth_pad(wide)
    pre = convolve(padded, kernel_one, forward)
    act = jnp.where(pre > 0, pre, leak_slope * pre).astype(jnp.bfloat16)
    pooled = pooling(act).astype(jnp.bfloat16)
    pooled_rimmed = extended(packing(pooled), (("tx", 1), ("ty", 2)), 1)
    pooled_pad = depth_pad(unpack(pooled_rimmed, CH))
    features = packing(convolve(pooled_pad, kernel_two, forward).astype(jnp.bfloat16))
    slab_two = convolve(pooled_pad, grads, weight_form)
    grad_pad = depth_pad(grad_rim)
    flipped = kernel_two[:, :, ::-1, ::-1, ::-1]
    back_pooled = convolve(grad_pad, flipped, backward).astype(jnp.bfloat16)
    slope = jnp.where(pre > 0, 1.0, leak_slope).astype(jnp.float32)
    back_pre = (upsample(back_pooled.astype(jnp.float32)) * 0.125 * slope).astype(jnp.bfloat16)
    slab_one = convolve(padded, back_pre, weight_form)
    replicas = lax.axis_size("rep")
    tile_one, tile_two = lax.psum((slab_one, slab_two), ("tx", "ty"))
    total_one, total_two = (
        lax.psum(tile_one.astype(jnp.bfloat16), "rep").astype(jnp.float32),
        lax.psum(tile_two.astype(jnp.bfloat16), "rep").astype(jnp.float32),
    )
    return (features, total_one / replicas, total_two / replicas)


def solution(mesh):
    in_specs = (P("rep", "tx", "ty", None), P(), P(), P("rep", "tx", "ty", None))
    out_specs = (P("rep", "tx", "ty", None), P(), P())
    return jax.shard_map(
        on_device, mesh=mesh, in_specs=in_specs, out_specs=out_specs, check_vma=False
    )
```

profile of v0, /device:TPU:0, one launch (start us, length us, event | category | flops | bytes accessed | tf_op | source)
XLA Modules:
  0.0 1262.0 jit_solution(5296581193335295249)
XLA Ops:
  2.2 3.3 collective-permute-start
  8.7 3.4 collective-permute-start.9
  13.6 7.6 copy.227
  31.6 3.0 collective-permute-start.11
  39.0 4.1 copy.233
  44.7 15.7 %copy.199 = bf16[34,1,8,11,4,32]{2,4,3,0,5,1:T(4,128)(2,1)} copy(bf16[34,1,8,11,4,32]{0,5,4,3,2,1:T(8,128)(2,1)S(1)} %fusion.23) | data formatting | bytes 1531904 | tf_op jit(solution)/shard_map/conv_general_dilated | solution.py:25
  60.4 79.3 %fusion.4 = f32[32,32,8,9,16]{4,2,3,1,0:T(8,128)} fusion(bf16[16,4,3,3,3]{0,1,4,3,2:T(4,128)(2,1)S(1)} %copy-done.13, bf16[34,1,8,11,4,32]{2,4,3,0,5,1:T(4,128)(2,1)} %copy.199), kind=kOutput, calls=%fused_computation.8 | convolution fusion | flops 249495552 | bytes 5488000 | tf_op jit(solution)/shard_map/conv_general_dilated | solution.py:25
  139.7 27.7 %copy.200 = f32[32,32,8,9,16]{1,4,3,2,0:T(8,128)} copy(f32[32,32,8,9,16]{4,2,3,1,0:T(8,128)} %fusion.4) | data formatting | bytes 9437184 | tf_op jit(solution)/shard_map/conv_general_dilated | solution.py:25
  167.4 17.8 %compare_select_fusion = (f32[32,32,8,9,16]{1,4,3,2,0:T(8,128)}, bf16[32,32,8,9,16]{1,4,3,2,0:T(8,128)(2,1)}) fusion(f32[32,32,8,9,16]{1,4,3,2,0:T(8,128)} %copy.200, pred[8,9]{1,0:T(8,128)(4,1)S(1)} %copy-done.12), kind=kLoop, calls=%fused_computation.5 | loop fusion | flops 7077888 | bytes 11796552 | tf_op jit(solution)/shard_map/jit(_where)/select_n | solution.py:75
  185.2 11.3 convert_bitcast_fusion
  196.5 30.0 %copy.201 = f32[1,16,32,32,64]{1,4,3,2,0:T(8,128)} copy(f32[1,16,32,32,64]{3,1,4,2,0:T(8,128)} %convert_bitcast_fusion) | data formatting | bytes 8388608 | tf_op jit(solution)/shard_map/reshape | solution.py:36
  226.5 25.2 %reduce_sum.9 = f32[16,16,16,32]{0,3,2,1:T(8,128)} reduce(f32[16,16,2,16,2,32,2]{0,6,5,4,3,2,1:T(2,128)} %bitcast.52, f32[]{:T(128)} %constant.5.clone.1), dimensions={2,4,6}, to_apply=%region_0.1 | reduce | flops 917504 | bytes 4718596 | tf_op jit(solution)/shard_map/reduce_sum | solution.py:37
  251.7 2.7 fusion.24
  255.6 11.7 slice.71
  269.2 3.8 collective-permute-start.5
  273.0 30.0 %copy.232 = f32[32,32,1,64,16]{4,3,1,0,2:T(8,128)} copy(f32[32,32,1,64,16]{1,4,3,0,2:T(8,128)} %slice.71) | data formatting | bytes 8388608
  302.9 65.3 %copy.223 = bf16[1,34,66,4,32]{3,0,2,1,4:T(2,128)(2,1)} copy(bf16[1,34,66,4,32]{2,4,3,1,0:T(8,128)(2,1)S(1)} %bitcast.67) | data formatting | bytes 1148928 | tf_op jit(solution)/shard_map/reshape | solution.py:48
  371.8 3.5 pad_maximum_fusion.2
  375.3 6.2 copy.234
  383.8 5.9 copy.219
  391.4 7.8 convert_multiply_fusion
  401.7 16.6 %broadcast_in_dim.12 = f32[16,16,2,16,2,32,2]{0,6,5,4,3,2,1:T(2,128)} broadcast(f32[16,16,16,32]{0,3,2,1:T(8,128)S(1)} %copy.221), dimensions={0,1,3,5} | broadcast | bytes 4718592 | tf_op jit(solution)/shard_map/broadcast_in_dim | solution.py:42
  418.3 27.8 %fusion = bf16[1,16,32,32,64]{1,4,3,2,0:T(8,128)(2,1)} fusion(f32[1,16,32,32,64]{1,4,3,2,0:T(8,128)} %bitcast.53, f32[32,32,1,64,16]{4,3,1,0,2:T(8,128)} %copy.232), kind=kLoop, calls=%fused_computation.1 | loop fusion | flops 2097152 | bytes 10485760 | tf_op jit(solution)/shard_map/convert_element_type | solution.py:76
  451.7 374.3 %fusion.1 = f32[16,4,3,3,3]{0,1,4,3,2:T(4,128)} fusion(bf16[1,34,66,4,32]{3,0,2,1,4:T(2,128)(2,1)} %copy.223, bf16[1,16,32,32,64]{1,4,3,2,0:T(8,128)(2,1)} %fusion), kind=kOutput, calls=%fused_computation.2 | convolution fusion | flops 221773824 | bytes 2678528 | tf_op jit(solution)/shard_map/conv_general_dilated | solution.py:25
  832.1 5.2 copy.207
  839.4 7.2 copy.209
  848.3 7.6 select_convert_fusion.1
  856.9 2.9 copy.211
  862.0 9.7 copy.226
  871.7 48.2 %fusion.43 = f32[16,16,3,3,3]{0,1,4,3,2:T(8,128)S(1)} fusion(bf16[1,18,34,16,16]{3,0,2,1,4:T(2,128)(2,1)} %copy.226, bf16[1,16,32,16,16]{3,0,2,1,4:T(2,128)(2,1)} %copy.227), kind=kOutput, calls=%fused_computation.59 | convolution fusion | flops 108527616 | bytes 603136 | tf_op jit(solution)/shard_map/conv_general_dilated | solution.py:25
  920.0 331.5 %all-reduce = (bf16[16,4,3,3,3]{0,1,4,3,2:T(4,128)(2,1)S(1)}, bf16[16,16,3,3,3]{0,1,4,3,2:T(8,128)(2,1)S(1)}) all-reduce(f32[16,4,3,3,3]{0,1,4,3,2:T(4,128)S(1)} %copy-done.11, f32[16,16,3,3,3]{0,1,4,3,2:T(8,128)S(1)} %fusion.43), channel_id=1, replica_groups=mesh['rep'=2,'tx'=8,'ty'=8] {'tx','ty'}, use_global_device_ids=true, to_apply=%region_1.2 | all-reduce | flops 8640 | bytes 51840 | tf_op jit(solution)/shard_map/psum | solution.py:79
  1251.5 8.8 all-reduce.1
  (97 shorter events, 55.7 us)
Async XLA Ops:
  0.6 390.7 %copy-start = (bf16[16,16,3,3,3]{1,0,4,3,2:T(8,128)(2,1)S(1)}, bf16[16,16,3,3,3]{1,0,4,3,2:T(8,128)(2,1)}, u32[]{:S(2)}) copy-start(bf16[16,16,3,3,3]{1,0,4,3,2:T(8,128)(2,1)} %param.6) | copy-start | bytes 41476
  2.2 19.0 %collective-permute-start = (bf16[1,1,64,128]{2,3,1,0:T(8,128)(2,1)S(1)}, bf16[1,1,64,128]{2,3,1,0:T(8,128)(2,1)S(1)}, u32[]{:S(2)}, u32[]{:S(2)}) collective-permute-start(bf16[1,1,64,128]{2,3,1,0:T(8,128)(2,1)S(1)} %get-tuple-element.36), channel_id=1, source_target_pairs={{0,8},{8,16},{16,24},{24,32},{32,40},{40,48},{48,56},{56,0},{1,9},... | collective-permute-start | bytes 49160 | tf_op jit(solution)/shard_map/ppermute | solution.py:18
  5.6 15.7 %collective-permute-start.1 = (bf16[1,1,64,128]{2,3,1,0:T(8,128)(2,1)S(1)}, bf16[1,1,64,128]{2,3,1,0:T(8,128)(2,1)S(1)}, u32[]{:S(2)}, u32[]{:S(2)}) collective-permute-start(bf16[1,1,64,128]{2,3,1,0:T(8,128)(2,1)S(1)} %get-tuple-element.37), channel_id=1, source_target_pairs={{8,0},{16,8},{24,16},{32,24},{40,32},{48,40},{56,48},{0,56},{9,1},... | collective-permute-start | bytes 49160 | tf_op jit(solution)/shard_map/ppermute | solution.py:19
  8.7 17.8 %collective-permute-start.9 = (bf16[1,1,32,256]{3,2,1,0:T(8,128)(2,1)S(1)}, bf16[1,1,32,256]{3,2,1,0:T(8,128)(2,1)S(1)}, u32[]{:S(2)}, u32[]{:S(2)}) collective-permute-start(bf16[1,1,32,256]{3,2,1,0:T(8,128)(2,1)S(1)} %get-tuple-element.40), channel_id=1, source_target_pairs={{8,0},{16,8},{24,16},{32,24},{40,32},{48,40},{56,48},{0,56},{9,1},... | collective-permute-start | bytes 49160 | tf_op jit(solution)/shard_map/ppermute | solution.py:19
  12.0 10.0 collective-permute-start.8
  21.2 0.9 copy-start.7
  22.2 0.7 copy-start.8
  23.9 11.3 collective-permute-start.3
  26.4 8.1 collective-permute-start.2
  31.6 338.1 %collective-permute-start.11 = (bf16[1,18,1,256]{3,1,2,0:T(8,128)(2,1)}, bf16[1,18,1,256]{3,1,2,0:T(8,128)(2,1)}, u32[]{:S(2)}, u32[]{:S(2)}) collective-permute-start(bf16[1,18,1,256]{3,1,2,0:T(8,128)(2,1)} %copy.231), channel_id=1, source_target_pairs={{1,0},{2,1},{3,2},{4,3},{5,4},{6,5},{7,6},{0,7},{9,8},{10,9},{11,1... | collective-permute-start | bytes 27656 | tf_op jit(solution)/shard_map/ppermute | solution.py:19
  34.5 333.7 %collective-permute-start.10 = (bf16[1,18,1,256]{3,1,2,0:T(8,128)(2,1)}, bf16[1,18,1,256]{3,1,2,0:T(8,128)(2,1)}, u32[]{:S(2)}, u32[]{:S(2)}) collective-permute-start(bf16[1,18,1,256]{3,1,2,0:T(8,128)(2,1)} %copy.230), channel_id=1, source_target_pairs={{0,1},{1,2},{2,3},{3,4},{4,5},{5,6},{6,7},{7,0},{8,9},{9,10},{10,1... | collective-permute-start | bytes 27656 | tf_op jit(solution)/shard_map/ppermute | solution.py:18
  39.0 4.8 copy-start.4
  44.7 15.7 %copy-start.13 = (bf16[16,4,3,3,3]{0,1,4,3,2:T(4,128)(2,1)S(1)}, bf16[16,4,3,3,3]{0,1,4,3,2:T(4,128)(2,1)}, u32[]{:S(2)}) copy-start(bf16[16,4,3,3,3]{0,1,4,3,2:T(4,128)(2,1)} %param.5) | copy-start | bytes 10372
  139.7 27.7 %copy-start.12 = (pred[8,9]{1,0:T(8,128)(4,1)S(1)}, pred[8,9]{1,0:T(8,128)(4,1)}, u32[]{:S(2)}) copy-start(pred[8,9]{1,0:T(8,128)(4,1)} %constant.34) | copy-start | bytes 220
  255.6 11.7 copy-start.1
  267.3 178.8 %collective-permute-start.4 = (bf16[1,1,32,256]{2,3,1,0:T(8,128)(2,1)S(1)}, bf16[1,1,32,256]{2,3,1,0:T(8,128)(2,1)S(1)}, u32[]{:S(2)}, u32[]{:S(2)}) collective-permute-start(bf16[1,1,32,256]{2,3,1,0:T(8,128)(2,1)S(1)} %get-tuple-element.34), channel_id=1, source_target_pairs={{0,8},{8,16},{16,24},{24,32},{32,40},{40,48},{48,56},{56,0},{1,9},... | collective-permute-start | bytes 49160 | tf_op jit(solution)/shard_map/ppermute | solution.py:18
  269.2 33.7 %copy-start.5 = (bf16[1,34,66,128]{2,3,1,0:T(8,128)(2,1)S(1)}, bf16[1,34,66,128]{2,3,1,0:T(8,128)(2,1)}, u32[]{:S(2)}) copy-start(bf16[1,34,66,128]{2,3,1,0:T(8,128)(2,1)} %copy-done.4) | copy-start | bytes 1723396
  269.2 176.9 %collective-permute-start.5 = (bf16[1,1,32,256]{2,3,1,0:T(8,128)(2,1)S(1)}, bf16[1,1,32,256]{2,3,1,0:T(8,128)(2,1)S(1)}, u32[]{:S(2)}, u32[]{:S(2)}) collective-permute-start(bf16[1,1,32,256]{2,3,1,0:T(8,128)(2,1)S(1)} %get-tuple-element.35), channel_id=1, source_target_pairs={{8,0},{16,8},{24,16},{32,24},{40,32},{48,40},{56,48},{0,56},{9,1},... | collective-permute-start | bytes 49160 | tf_op jit(solution)/shard_map/ppermute | solution.py:19
  368.2 3.6 copy-start.6
  383.8 7.6 copy-start.14
  418.3 27.8 %copy-start.2 = (bf16[1,16,32,16,16]{2,4,3,1,0:T(8,128)(2,1)S(1)}, bf16[1,16,32,16,16]{2,4,3,1,0:T(8,128)(2,1)}, u32[]{:S(2)}) copy-start(bf16[1,16,32,16,16]{2,4,3,1,0:T(8,128)(2,1)} %copy-done.1) | copy-start | bytes 786436
  446.1 0.8 copy-start.9
  446.1 0.8 copy-start.10
  449.3 378.2 %collective-permute-start.7 = (bf16[1,18,1,256]{3,1,2,0:T(8,128)(2,1)}, bf16[1,18,1,256]{3,1,2,0:T(8,128)(2,1)}, u32[]{:S(2)}, u32[]{:S(2)}) collective-permute-start(bf16[1,18,1,256]{3,1,2,0:T(8,128)(2,1)} %copy.204), channel_id=1, source_target_pairs={{1,0},{2,1},{3,2},{4,3},{5,4},{6,5},{7,6},{0,7},{9,8},{10,9},{11,1... | collective-permute-start | bytes 27656 | tf_op jit(solution)/shard_map/ppermute | solution.py:19
  451.7 374.3 %collective-permute-start.6 = (bf16[1,18,1,256]{3,1,2,0:T(8,128)(2,1)}, bf16[1,18,1,256]{3,1,2,0:T(8,128)(2,1)}, u32[]{:S(2)}, u32[]{:S(2)}) collective-permute-start(bf16[1,18,1,256]{3,1,2,0:T(8,128)(2,1)} %copy.203), channel_id=1, source_target_pairs={{0,1},{1,2},{2,3},{3,4},{4,5},{5,6},{6,7},{7,0},{8,9},{9,10},{10,1... | collective-permute-start | bytes 27656 | tf_op jit(solution)/shard_map/ppermute | solution.py:18
  826.0 3.7 copy-start.3
  839.4 8.9 copy-start.15
  871.7 48.2 %copy-start.11 = (f32[16,4,3,3,3]{0,1,4,3,2:T(4,128)S(1)}, f32[16,4,3,3,3]{0,1,4,3,2:T(4,128)}, u32[]{:S(2)}) copy-start(f32[16,4,3,3,3]{0,1,4,3,2:T(4,128)} %fusion.1) | copy-start | bytes 20740
where the time goes:
time: 1270 us; the launch traced here: 1260 us
  matrix products  517 us (41%)
  blocking collectives  340 us (27%)
  local copies, waits for them, and re-layouts  285 us (22%)
  other arithmetic  95 us (7%)
  starting transfers between devices  22.8 us (2%)
    conv_general_dilated x5, matrix products, convolve(): lax.conv_general_dilated(lhs, rhs, (1, 1, 1), 'VALID', dimension_numbers=...  517 us
    psum x1, blocking collectives, on_device(): tile_one, tile_two = lax.psum((slab_one, slab_two), ('tx', 'ty'))  332 us
    reshape x7, local copies, waits for them, and re-layouts, unpack(): field.reshape(s, x, y, channels, merged // channels)  92.8 us
    conv_general_dilated x7, local copies, waits for them, and re-layouts, convolve(): lax.conv_general_dilated(lhs, rhs, (1, 1, 1), 'VALID', dimension_numbers=...  59.8 us
    unnamed x43, local copies, waits for them, and re-layouts  48.5 us
    reshape x1, local copies, waits for them, and re-layouts, pooling(): field.astype(jnp.float32).reshape(s, c, d // 2, 2, x // 2, 2, y // 2, 2)  30 us
    convert_element_type x1, other arithmetic, on_device(): (upsample(back_pooled.astype(jnp.float32)) * 0.125 * slope).astype(jnp.bf...  27.8 us
  transfers between devices with their start and end apart: 12, of which 0 were waited for; matrix products, arithmetic and copies ran while one was open for 63% of the time, Pallas kernels for 0%

commit v1 on v0

--- a/solution.py
+++ b/solution.py
@@ -76,7 +76,7 @@
     back_pre = (upsample(back_pooled.astype(jnp.float32)) * 0.125 * slope).astype(jnp.bfloat16)
     slab_one = convolve(padded, back_pre, weight_form)
     replicas = lax.axis_size("rep")
-    tile_one, tile_two = lax.psum((slab_one, slab_two), ("tx", "ty"))
+    tile_one, tile_two = lax.psum(lax.psum((slab_one, slab_two), "tx"), "ty")
     total_one, total_two = (
         lax.psum(tile_one.astype(jnp.bfloat16), "rep").astype(jnp.float32),
         lax.psum(tile_two.astype(jnp.bfloat16), "rep").astype(jnp.float32),

time: 1270 us -> 1010 us (0.80)
  blocking collectives: 340 us -> 78.2 us
    psum x1 -> x2, blocking collectives: 332 us -> 69.6 us  [on_device(): tile_one, tile_two = lax.psum(lax.psum((slab_one, slab_two), 'tx'), 'ty')]
  transfers between devices with their start and end apart: 12 -> 12, of which waited for: 0 -> 0; matrix products, arithmetic and copies ran while one was open for 63% -> 80% of each run, Pallas kernels for 0% -> 0%
where the time goes in v1:
time: 1010 us; the launch traced here: 1000 us
  matrix products  517 us (51%)
  local copies, waits for them, and re-layouts  285 us (28%)
  other arithmetic  94.9 us (9%)
  blocking collectives  78.2 us (8%)
  starting transfers between devices  22.8 us (2%)
    conv_general_dilated x5, matrix products, convolve(): lax.conv_general_dilated(lhs, rhs, (1, 1, 1), 'VALID', dimension_numbers=...  517 us
    reshape x7, local copies, waits for them, and re-layouts, unpack(): field.reshape(s, x, y, channels, merged // channels)  92.7 us
    psum x2, blocking collectives, on_device(): tile_one, tile_two = lax.psum(lax.psum((slab_one, slab_two), 'tx'), 'ty')  69.6 us
    conv_general_dilated x7, local copies, waits for them, and re-layouts, convolve(): lax.conv_general_dilated(lhs, rhs, (1, 1, 1), 'VALID', dimension_numbers=...  59.8 us
    unnamed x43, local copies, waits for them, and re-layouts  48.5 us
    reshape x1, local copies, waits for them, and re-layouts, pooling(): field.astype(jnp.float32).reshape(s, c, d // 2, 2, x // 2, 2, y // 2, 2)  30 us
    convert_element_type x1, other arithmetic, on_device(): (upsample(back_pooled.astype(jnp.float32)) * 0.125 * slope).astype(jnp.bf...  27.8 us
    reduce_sum x1, other arithmetic, pooling(): return jnp.mean(blocks, axis=(3, 5, 7))  25.2 us
  transfers between devices with their start and end apart: 12, of which 0 were waited for; matrix products, arithmetic and copies ran while one was open for 80% of the time, Pallas kernels for 0%

profile of v1, /device:TPU:0, one launch (start us, length us, event | category | flops | bytes accessed | tf_op | source)
XLA Modules:
  0.0 999.7 jit_solution(4551434273645573837)
XLA Ops:
  2.2 3.3 collective-permute-start
  8.7 3.4 collective-permute-start.9
  13.6 7.5 copy.227
  31.5 3.0 collective-permute-start.11
  39.0 4.1 copy.233
  44.6 15.7 %copy.199 = bf16[34,1,8,11,4,32]{2,4,3,0,5,1:T(4,128)(2,1)} copy(bf16[34,1,8,11,4,32]{0,5,4,3,2,1:T(8,128)(2,1)S(1)} %fusion.23) | data formatting | bytes 1531904 | tf_op jit(solution)/shard_map/conv_general_dilated | solution.py:25
  60.3 79.3 %fusion.4 = f32[32,32,8,9,16]{4,2,3,1,0:T(8,128)} fusion(bf16[16,4,3,3,3]{0,1,4,3,2:T(4,128)(2,1)S(1)} %copy-done.13, bf16[34,1,8,11,4,32]{2,4,3,0,5,1:T(4,128)(2,1)} %copy.199), kind=kOutput, calls=%fused_computation.8 | convolution fusion | flops 249495552 | bytes 5488000 | tf_op jit(solution)/shard_map/conv_general_dilated | solution.py:25
  139.6 27.7 %copy.200 = f32[32,32,8,9,16]{1,4,3,2,0:T(8,128)} copy(f32[32,32,8,9,16]{4,2,3,1,0:T(8,128)} %fusion.4) | data formatting | bytes 9437184 | tf_op jit(solution)/shard_map/conv_general_dilated | solution.py:25
  167.3 17.7 %compare_select_fusion = (f32[32,32,8,9,16]{1,4,3,2,0:T(8,128)}, bf16[32,32,8,9,16]{1,4,3,2,0:T(8,128)(2,1)}) fusion(f32[32,32,8,9,16]{1,4,3,2,0:T(8,128)} %copy.200, pred[8,9]{1,0:T(8,128)(4,1)S(1)} %copy-done.12), kind=kLoop, calls=%fused_computation.5 | loop fusion | flops 7077888 | bytes 11796552 | tf_op jit(solution)/shard_map/jit(_where)/select_n | solution.py:75
  185.0 11.3 %convert_bitcast_fusion = f32[1,16,32,32,64]{3,1,4,2,0:T(8,128)} fusion(bf16[32,32,1,72,16]{1,4,3,0,2:T(8,128)(2,1)} %bitcast.55), kind=kLoop, calls=%fused_computation.7 | loop fusion | flops 1048576 | bytes 6291456 | tf_op jit(solution)/shard_map/reshape | solution.py:36
  196.3 30.0 %copy.201 = f32[1,16,32,32,64]{1,4,3,2,0:T(8,128)} copy(f32[1,16,32,32,64]{3,1,4,2,0:T(8,128)} %convert_bitcast_fusion) | data formatting | bytes 8388608 | tf_op jit(solution)/shard_map/reshape | solution.py:36
  226.3 25.2 %reduce_sum.9 = f32[16,16,16,32]{0,3,2,1:T(8,128)} reduce(f32[16,16,2,16,2,32,2]{0,6,5,4,3,2,1:T(2,128)} %bitcast.52, f32[]{:T(128)} %constant.5.clone.1), dimensions={2,4,6}, to_apply=%region_0.1 | reduce | flops 917504 | bytes 4718596 | tf_op jit(solution)/shard_map/reduce_sum | solution.py:37
  255.5 11.7 %slice.71 = f32[32,32,1,64,16]{1,4,3,0,2:T(8,128)} slice(f32[32,32,1,72,16]{1,4,3,0,2:T(8,128)} %bitcast.54), slice={[0:32], [0:32], [0:1], [0:64], [0:16]} | slice | bytes 8388608 | tf_op jit(solution)/shard_map/jit(_where)/select_n | solution.py:75
  269.0 3.8 collective-permute-start.5
  272.8 30.0 %copy.232 = f32[32,32,1,64,16]{4,3,1,0,2:T(8,128)} copy(f32[32,32,1,64,16]{1,4,3,0,2:T(8,128)} %slice.71) | data formatting | bytes 8388608
  302.8 65.2 %copy.223 = bf16[1,34,66,4,32]{3,0,2,1,4:T(2,128)(2,1)} copy(bf16[1,34,66,4,32]{2,4,3,1,0:T(8,128)(2,1)S(1)} %bitcast.67) | data formatting | bytes 1148928 | tf_op jit(solution)/shard_map/reshape | solution.py:48
  371.6 3.4 pad_maximum_fusion.2
  375.1 6.2 copy.234
  383.6 5.9 copy.219
  391.2 7.8 convert_multiply_fusion
  401.5 16.7 %broadcast_in_dim.12 = f32[16,16,2,16,2,32,2]{0,6,5,4,3,2,1:T(2,128)} broadcast(f32[16,16,16,32]{0,3,2,1:T(8,128)S(1)} %copy.221), dimensions={0,1,3,5} | broadcast | bytes 4718592 | tf_op jit(solution)/shard_map/broadcast_in_dim | solution.py:42
  418.2 27.8 %fusion = bf16[1,16,32,32,64]{1,4,3,2,0:T(8,128)(2,1)} fusion(f32[1,16,32,32,64]{1,4,3,2,0:T(8,128)} %bitcast.53, f32[32,32,1,64,16]{4,3,1,0,2:T(8,128)} %copy.232), kind=kLoop, calls=%fused_computation.1 | loop fusion | flops 2097152 | bytes 10485760 | tf_op jit(solution)/shard_map/convert_element_type | solution.py:76
  451.5 374.3 %fusion.1 = f32[16,4,3,3,3]{0,1,4,3,2:T(4,128)} fusion(bf16[1,34,66,4,32]{3,0,2,1,4:T(2,128)(2,1)} %copy.223, bf16[1,16,32,32,64]{1,4,3,2,0:T(8,128)(2,1)} %fusion), kind=kOutput, calls=%fused_computation.2 | convolution fusion | flops 221773824 | bytes 2678528 | tf_op jit(solution)/shard_map/conv_general_dilated | solution.py:25
  831.9 5.2 copy.207
  839.3 7.2 copy.209
  848.1 7.6 select_convert_fusion.1
  856.7 2.9 copy.211
  861.8 9.7 copy.226
  871.5 48.2 %fusion.43 = f32[16,16,3,3,3]{0,1,4,3,2:T(8,128)S(1)} fusion(bf16[1,18,34,16,16]{3,0,2,1,4:T(2,128)(2,1)} %copy.226, bf16[1,16,32,16,16]{3,0,2,1,4:T(2,128)(2,1)} %copy.227), kind=kOutput, calls=%fused_computation.59 | convolution fusion | flops 108527616 | bytes 603136 | tf_op jit(solution)/shard_map/conv_general_dilated | solution.py:25
  919.8 43.0 %all-reduce.1 = (f32[16,4,3,3,3]{0,1,4,3,2:T(4,128)S(1)}, f32[16,16,3,3,3]{0,1,4,3,2:T(8,128)S(1)}) all-reduce(f32[16,4,3,3,3]{0,1,4,3,2:T(4,128)S(1)} %copy-done.11, f32[16,16,3,3,3]{0,1,4,3,2:T(8,128)S(1)} %fusion.43), channel_id=1, replica_groups=mesh['rep'=2,'tx'=8,'ty'=8] {'tx'}, use_global_device_ids=true, to_apply=%region_1.2 | all-reduce | flops 8640 | bytes 69120 | tf_op jit(solution)/shard_map/psum | solution.py:79
  962.8 26.6 %all-reduce = (bf16[16,4,3,3,3]{0,1,4,3,2:T(4,128)(2,1)S(1)}, bf16[16,16,3,3,3]{0,1,4,3,2:T(8,128)(2,1)S(1)}) all-reduce(f32[16,4,3,3,3]{0,1,4,3,2:T(4,128)S(1)} %get-tuple-element.26, f32[16,16,3,3,3]{0,1,4,3,2:T(8,128)S(1)} %get-tuple-element.27), channel_id=1, replica_groups=mesh['rep'=2,'tx'=8,'ty'=8] {'ty'}, use_global_device_ids=true, to_apply=%region_2.3 | all-reduce | flops 8640 | bytes 51840 | tf_op jit(solution)/shard_map/psum | solution.py:79
  989.4 8.6 all-reduce.2
  (98 shorter events, 58.4 us)
Async XLA Ops:
  0.6 390.5 %copy-start = (bf16[16,16,3,3,3]{1,0,4,3,2:T(8,128)(2,1)S(1)}, bf16[16,16,3,3,3]{1,0,4,3,2:T(8,128)(2,1)}, u32[]{:S(2)}) copy-start(bf16[16,16,3,3,3]{1,0,4,3,2:T(8,128)(2,1)} %param.6) | copy-start | bytes 41476
  2.2 19.0 %collective-permute-start = (bf16[1,1,64,128]{2,3,1,0:T(8,128)(2,1)S(1)}, bf16[1,1,64,128]{2,3,1,0:T(8,128)(2,1)S(1)}, u32[]{:S(2)}, u32[]{:S(2)}) collective-permute-start(bf16[1,1,64,128]{2,3,1,0:T(8,128)(2,1)S(1)} %get-tuple-element.38), channel_id=1, source_target_pairs={{0,8},{8,16},{16,24},{24,32},{32,40},{40,48},{48,56},{56,0},{1,9},... | collective-permute-start | bytes 49160 | tf_op jit(solution)/shard_map/ppermute | solution.py:18
  5.6 15.6 %collective-permute-start.1 = (bf16[1,1,64,128]{2,3,1,0:T(8,128)(2,1)S(1)}, bf16[1,1,64,128]{2,3,1,0:T(8,128)(2,1)S(1)}, u32[]{:S(2)}, u32[]{:S(2)}) collective-permute-start(bf16[1,1,64,128]{2,3,1,0:T(8,128)(2,1)S(1)} %get-tuple-element.39), channel_id=1, source_target_pairs={{8,0},{16,8},{24,16},{32,24},{40,32},{48,40},{56,48},{0,56},{9,1},... | collective-permute-start | bytes 49160 | tf_op jit(solution)/shard_map/ppermute | solution.py:19
  8.7 17.7 %collective-permute-start.9 = (bf16[1,1,32,256]{3,2,1,0:T(8,128)(2,1)S(1)}, bf16[1,1,32,256]{3,2,1,0:T(8,128)(2,1)S(1)}, u32[]{:S(2)}, u32[]{:S(2)}) collective-permute-start(bf16[1,1,32,256]{3,2,1,0:T(8,128)(2,1)S(1)} %get-tuple-element.42), channel_id=1, source_target_pairs={{8,0},{16,8},{24,16},{32,24},{40,32},{48,40},{56,48},{0,56},{9,1},... | collective-permute-start | bytes 49160 | tf_op jit(solution)/shard_map/ppermute | solution.py:19
  12.0 9.9 collective-permute-start.8
  21.2 0.9 copy-start.7
  22.1 0.7 copy-start.8
  23.8 11.3 %collective-permute-start.3 = (bf16[1,34,1,128]{3,1,2,0:T(8,128)(2,1)S(1)}, bf16[1,34,1,128]{3,1,2,0:T(8,128)(2,1)S(1)}, u32[]{:S(2)}, u32[]{:S(2)}) collective-permute-start(bf16[1,34,1,128]{3,1,2,0:T(8,128)(2,1)S(1)} %copy.195), channel_id=1, source_target_pairs={{1,0},{2,1},{3,2},{4,3},{5,4},{6,5},{7,6},{0,7},{9,8},{10,9},{11,1... | collective-permute-start | bytes 26120 | tf_op jit(solution)/shard_map/ppermute | solution.py:19
  26.4 8.1 collective-permute-start.2
  31.5 337.9 %collective-permute-start.11 = (bf16[1,18,1,256]{3,1,2,0:T(8,128)(2,1)}, bf16[1,18,1,256]{3,1,2,0:T(8,128)(2,1)}, u32[]{:S(2)}, u32[]{:S(2)}) collective-permute-start(bf16[1,18,1,256]{3,1,2,0:T(8,128)(2,1)} %copy.231), channel_id=1, source_target_pairs={{1,0},{2,1},{3,2},{4,3},{5,4},{6,5},{7,6},{0,7},{9,8},{10,9},{11,1... | collective-permute-start | bytes 27656 | tf_op jit(solution)/shard_map/ppermute | solution.py:19
  34.5 333.5 %collective-permute-start.10 = (bf16[1,18,1,256]{3,1,2,0:T(8,128)(2,1)}, bf16[1,18,1,256]{3,1,2,0:T(8,128)(2,1)}, u32[]{:S(2)}, u32[]{:S(2)}) collective-permute-start(bf16[1,18,1,256]{3,1,2,0:T(8,128)(2,1)} %copy.230), channel_id=1, source_target_pairs={{0,1},{1,2},{2,3},{3,4},{4,5},{5,6},{6,7},{7,0},{8,9},{9,10},{10,1... | collective-permute-start | bytes 27656 | tf_op jit(solution)/shard_map/ppermute | solution.py:18
  39.0 4.8 copy-start.4
  44.6 15.7 %copy-start.13 = (bf16[16,4,3,3,3]{0,1,4,3,2:T(4,128)(2,1)S(1)}, bf16[16,4,3,3,3]{0,1,4,3,2:T(4,128)(2,1)}, u32[]{:S(2)}) copy-start(bf16[16,4,3,3,3]{0,1,4,3,2:T(4,128)(2,1)} %param.5) | copy-start | bytes 10372
  139.6 27.7 %copy-start.12 = (pred[8,9]{1,0:T(8,128)(4,1)S(1)}, pred[8,9]{1,0:T(8,128)(4,1)}, u32[]{:S(2)}) copy-start(pred[8,9]{1,0:T(8,128)(4,1)} %constant.34) | copy-start | bytes 220
  255.4 11.7 %copy-start.1 = (bf16[1,16,32,16,16]{2,4,3,1,0:T(8,128)(2,1)}, bf16[1,16,32,16,16]{2,4,3,1,0:T(8,128)(2,1)S(1)}, u32[]{:S(2)}) copy-start(bf16[1,16,32,16,16]{2,4,3,1,0:T(8,128)(2,1)S(1)} %copy.202) | copy-start | bytes 786436
  267.2 178.8 %collective-permute-start.4 = (bf16[1,1,32,256]{2,3,1,0:T(8,128)(2,1)S(1)}, bf16[1,1,32,256]{2,3,1,0:T(8,128)(2,1)S(1)}, u32[]{:S(2)}, u32[]{:S(2)}) collective-permute-start(bf16[1,1,32,256]{2,3,1,0:T(8,128)(2,1)S(1)} %get-tuple-element.36), channel_id=1, source_target_pairs={{0,8},{8,16},{16,24},{24,32},{32,40},{40,48},{48,56},{56,0},{1,9},... | collective-permute-start | bytes 49160 | tf_op jit(solution)/shard_map/ppermute | solution.py:18
  269.0 33.8 %copy-start.5 = (bf16[1,34,66,128]{2,3,1,0:T(8,128)(2,1)S(1)}, bf16[1,34,66,128]{2,3,1,0:T(8,128)(2,1)}, u32[]{:S(2)}) copy-start(bf16[1,34,66,128]{2,3,1,0:T(8,128)(2,1)} %copy-done.4) | copy-start | bytes 1723396
  269.0 176.9 %collective-permute-start.5 = (bf16[1,1,32,256]{2,3,1,0:T(8,128)(2,1)S(1)}, bf16[1,1,32,256]{2,3,1,0:T(8,128)(2,1)S(1)}, u32[]{:S(2)}, u32[]{:S(2)}) collective-permute-start(bf16[1,1,32,256]{2,3,1,0:T(8,128)(2,1)S(1)} %get-tuple-element.37), channel_id=1, source_target_pairs={{8,0},{16,8},{24,16},{32,24},{40,32},{48,40},{56,48},{0,56},{9,1},... | collective-permute-start | bytes 49160 | tf_op jit(solution)/shard_map/ppermute | solution.py:19
  368.0 3.6 copy-start.6
  383.6 7.6 copy-start.14
  418.1 27.8 %copy-start.2 = (bf16[1,16,32,16,16]{2,4,3,1,0:T(8,128)(2,1)S(1)}, bf16[1,16,32,16,16]{2,4,3,1,0:T(8,128)(2,1)}, u32[]{:S(2)}) copy-start(bf16[1,16,32,16,16]{2,4,3,1,0:T(8,128)(2,1)} %copy-done.1) | copy-start | bytes 786436
  445.9 0.8 copy-start.9
  445.9 0.8 copy-start.10
  449.1 378.2 %collective-permute-start.7 = (bf16[1,18,1,256]{3,1,2,0:T(8,128)(2,1)}, bf16[1,18,1,256]{3,1,2,0:T(8,128)(2,1)}, u32[]{:S(2)}, u32[]{:S(2)}) collective-permute-start(bf16[1,18,1,256]{3,1,2,0:T(8,128)(2,1)} %copy.204), channel_id=1, source_target_pairs={{1,0},{2,1},{3,2},{4,3},{5,4},{6,5},{7,6},{0,7},{9,8},{10,9},{11,1... | collective-permute-start | bytes 27656 | tf_op jit(solution)/shard_map/ppermute | solution.py:19
  451.5 374.3 %collective-permute-start.6 = (bf16[1,18,1,256]{3,1,2,0:T(8,128)(2,1)}, bf16[1,18,1,256]{3,1,2,0:T(8,128)(2,1)}, u32[]{:S(2)}, u32[]{:S(2)}) collective-permute-start(bf16[1,18,1,256]{3,1,2,0:T(8,128)(2,1)} %copy.203), channel_id=1, source_target_pairs={{0,1},{1,2},{2,3},{3,4},{4,5},{5,6},{6,7},{7,0},{8,9},{9,10},{10,1... | collective-permute-start | bytes 27656 | tf_op jit(solution)/shard_map/ppermute | solution.py:18
  825.8 3.7 copy-start.3
  839.3 8.9 copy-start.15
  871.5 48.2 %copy-start.11 = (f32[16,4,3,3,3]{0,1,4,3,2:T(4,128)S(1)}, f32[16,4,3,3,3]{0,1,4,3,2:T(4,128)}, u32[]{:S(2)}) copy-start(f32[16,4,3,3,3]{0,1,4,3,2:T(4,128)} %fusion.1) | copy-start | bytes 20740
